TPU v7x, 32 devices: a whole 2x2x4 slice. The times are simulated.
32 devices in a mesh: section: 4 (over y, x), trial: 8 (over z, core).
Axes of the slice: x: 2, y: 2, z: 4, core: 2. Of those that a mesh axis runs over, the one named last changes fastest.
Arguments:
- spike_rates: bfloat16 [512, 16, 256], P(None, 'trial'), may hold values from -6 to 6
- first_preactivation: bfloat16 [1024, 16, 256], P('section', 'trial'), may hold values from -6 to 6
- second_preactivation: bfloat16 [1024, 16, 256], P('section', 'trial'), may hold values from -6 to 6
- output_gradient: bfloat16 [1024, 16, 256], P('section', 'trial'), may hold values from -0.29882812 to 0.29882812
- first_kernel: bfloat16 [3, 1024, 1024], P(None, None, 'section'), may hold values from -0.109375 to 0.109375
- second_kernel: bfloat16 [3, 1024, 1024], P(None, None, 'section'), may hold values from -0.109375 to 0.109375
- session_of: int32 [16], P('trial'), may hold values from 0 to 7, never falling along the last dimension, each value on 1 to 6 neighbouring positions
Outputs:
- readin_grad: bfloat16 [8, 512, 1024], P(None, 'trial', 'section')
Inputs may be any that keep to these rules, and one draw needn't show every extreme that they name: `session_of`: the trials of a session are consecutive; every session has 1 to 6 trials, and one has exactly 6.
All inputs are finite; a program needn't handle non-finite values.
Results may differ from a plain program's by a relative error of at most 0.017.
Values may be sent and summed in bfloat16 or wider, within the bound.
A program may use at most 64 MiB of HBM per device.

v0:
```python
import math

import jax
import jax.numpy as jnp
from jax import lax
from jax.sharding import PartitionSpec as P

FIRST_DILATION = 32
SECOND_DILATION = 64
MOST = 6


def gelu_slope(preact):
    values = preact.astype(jnp.float32)
    normal_cdf = 0.5 * (1.0 + lax.erf(values * (1.0 / math.sqrt(2.0))))
    density = jnp.exp(-0.5 * values * values) * (1.0 / math.sqrt(2.0 * math.pi))
    return normal_cdf + values * density


def shift_ahead(values, offset):
    padding = [(0, 0)] * (values.ndim - 1) + [(0, offset)]
    return jnp.pad(values[..., offset:], padding)


def tap_sum(weights, flow_grad, spacing):
    running = None
    for kernel_tap in range(3):
        term_tap = lax.dot_general(
            weights[kernel_tap],
            flow_grad,
            (((1,), (0,)), ((), ())),
            preferred_element_type=jnp.float32,
        )
        if kernel_tap > 0:
            term_tap = shift_ahead(term_tap, kernel_tap * spacing)
        running = term_tap if running is None else running + term_tap
    return running


def layer_backprop(upstream, preact, turned, spacing):
    flow_grad = (upstream.astype(jnp.float32) * gelu_slope(preact)).astype(jnp.bfloat16)
    back_sum = tap_sum(turned, lax.all_gather(flow_grad, "section", axis=0, tiled=True), spacing)
    return (upstream.astype(jnp.float32) + back_sum).astype(jnp.bfloat16)


def body(
    spike_rates,
    first_preactivation,
    second_preactivation,
    output_gradient,
    first_kernel,
    second_kernel,
    session_of,
):
    first_flipped_kernel, second_flipped_kernel = (
        lax.all_to_all(first_kernel, "section", split_axis=1, concat_axis=2, tiled=True),
        lax.all_to_all(second_kernel, "section", split_axis=1, concat_axis=2, tiled=True),
    )
    upstream_gradient = layer_backprop(
        output_gradient, second_preactivation, second_flipped_kernel, SECOND_DILATION
    )
    input_gradient = layer_backprop(
        upstream_gradient, first_preactivation, first_flipped_kernel, FIRST_DILATION
    )
    trial_shards = lax.axis_size("trial")
    neurons, trials, steps_count = spike_rates.shape
    neuron_blocks = spike_rates.reshape(trial_shards, neurons // trial_shards, trials, steps_count)
    partials = jnp.einsum(
        "jbil,cil->jibc", neuron_blocks, input_gradient, preferred_element_type=jnp.float32
    )
    arrived = lax.all_to_all(
        partials.astype(jnp.bfloat16), "trial", split_axis=0, concat_axis=0, tiled=True
    ).astype(partials.dtype)
    every_id = lax.all_gather(session_of, "trial", axis=0, tiled=True)
    total_trials = every_id.shape[0]
    flat_parts = arrived.reshape(total_trials, -1)
    session_list = jnp.arange(trial_shards, dtype=jnp.int32)
    first_trial = jnp.sum((every_id[None, :] < session_list[:, None]).astype(jnp.int32), axis=1)

    def add_offset(offset, running):
        position = first_trial + offset
        clipped = jnp.minimum(position, total_trials - 1)
        rows_here = jnp.take(flat_parts, clipped, axis=0)
        valid = (position < total_trials) & (jnp.take(every_id, clipped, axis=0) == session_list)
        return running + jnp.where(valid[:, None], rows_here, 0.0)

    start_sums = jnp.zeros((trial_shards, flat_parts.shape[1]), jnp.float32)
    summed = lax.fori_loop(0, MOST, add_offset, start_sums)
    return summed.reshape(trial_shards, neurons // trial_shards, input_gradient.shape[0]).astype(
        jnp.bfloat16
    )


def solution(mesh):
    in_specs = (
        P(None, "trial", None),
        P("section", "trial", None),
        P("section", "trial", None),
        P("section", "trial", None),
        P(None, None, "section"),
        P(None, None, "section"),
        P("trial"),
    )
    out_specs = P(None, "trial", "section")
    return jax.shard_map(body, mesh=mesh, in_specs=in_specs, out_specs=out_specs, check_vma=False)
```

profile of v0, /device:TPU:0, one launch (start us, length us, event | category | flops | bytes accessed | tf_op | source)
XLA Modules:
  0.0 140.1 jit_solution(10442838819830731775)
XLA Ops:
  6.5 1.2 copy.50
  7.8 1.1 copy.51
  8.9 1.0 fusion.13
  9.8 0.0 all-gather.3.cloned.1.call-update
  9.9 2.7 %copy.52 = bf16[3,1024,256]{2,0,1:T(4,128)(2,1)} copy(bf16[3,1024,256]{2,1,0:T(8,128)(2,1)S(1)} %copy-done.2) | data formatting | bytes 3145728 | tf_op args[5]
  12.6 5.3 %all-to-all-start = ((bf16[3,1024,256]{2,0,1:T(4,128)(2,1)}), bf16[3,1024,256]{2,0,1:T(4,128)(2,1)S(1)}, u32[]{:S(2)}, u32[]{:S(2)}) async-start(bf16[3,1024,256]{2,0,1:T(4,128)(2,1)} %copy.52), calls=%async_computation | async-start | bytes 4194304 | tf_op jit(solution)/shard_map/all_to_all | solution.py:57
  17.9 0.2 copy.54
  18.0 28.1 %all-to-all-done = bf16[3,1024,256]{2,0,1:T(4,128)(2,1)S(1)} async-done(((bf16[3,1024,256]{2,0,1:T(4,128)(2,1)}), bf16[3,1024,256]{2,0,1:T(4,128)(2,1)S(1)}, u32[]{:S(2)}, u32[]{:S(2)}) %all-to-all-start) | async-done | bytes 1572896 | tf_op jit(solution)/shard_map/all_to_all | solution.py:57
  46.1 1.5 %copy.77 = bf16[3,4,256,256]{3,1,2,0:T(4,128)(2,1)S(1)} copy(bf16[3,4,256,256]{3,0,2,1:T(4,128)(2,1)S(1)} %bitcast.86) | data formatting | bytes 3145728 | tf_op jit(solution)/shard_map/all_to_all | solution.py:57
  47.6 0.5 fusion.32
  48.1 0.4 reshape.105
  48.5 0.4 reshape.106
  48.9 0.4 reshape.104
  49.2 2.2 %all-gather.3.cloned.1.call-done = bf16[1024,2,256]{0,2,1:T(8,128)(2,1)} async-done(((bf16[256,2,256]{0,2,1:T(8,128)(2,1)}), bf16[1024,2,256]{0,2,1:T(8,128)(2,1)}) %all-gather.3.cloned.1.call-update) | async-done | bytes 1048592 | tf_op jit(solution)/shard_map/all_gather | solution.py:42
  51.4 1.8 %convolution_bitcast_fusion.4 = f32[256,2,256]{0,2,1:T(8,128)S(1)} fusion(bf16[1024,2,256]{0,2,1:T(8,128)(2,1)} %all-gather.3.cloned.1.call-done, bf16[256,1024,1]{1,0,2:T(8,128)(2,1)S(1)} %reshape.105), kind=kOutput, calls=%fused_computation.18 | convolution fusion | flops 268435456 | bytes 2097152 | tf_op jit(solution)/shard_map/dot_general | solution.py:28
  53.3 0.5 convolution_bitcast_fusion.3
  53.8 0.0 copy-start.3
  53.8 1.5 %fusion.29 = (bf16[256,2,256]{0,2,1:T(8,128)(2,1)}, f32[256,2,256]{0,2,1:T(8,128)}) fusion(bf16[256,2,256]{0,2,1:T(8,128)(2,1)S(1)} %copy.54, f32[256,2,128]{0,2,1:T(8,128)S(1)} %slice.54, f32[256,2,192]{0,2,1:T(8,128)S(1)} %slice.52, bf16[1024,2,256]{0,2,1:T(8,128)(2,1)S(1)} %copy-done.1, bf16[256,1024,1]{1,0,2:T(8,128)(2,1)S(1)} %reshape.104, ...), kind=kOutput, calls=%fused_computation.54 | convolution fusion | flops 270663680 | bytes 3538944 | tf_op jit(solution)/shard_map/dot_general | solution.py:28
  55.2 0.0 all-gather.5.cloned.1.call-update
  55.3 2.7 %copy.55 = bf16[3,1024,256]{2,0,1:T(4,128)(2,1)} copy(bf16[3,1024,256]{2,1,0:T(8,128)(2,1)S(1)} %copy-done.3) | data formatting | bytes 3145728 | tf_op args[4]
  58.0 3.7 %all-to-all-start.1 = ((bf16[3,1024,256]{2,0,1:T(4,128)(2,1)}), bf16[3,1024,256]{2,0,1:T(4,128)(2,1)S(1)}, u32[]{:S(2)}, u32[]{:S(2)}) async-start(bf16[3,1024,256]{2,0,1:T(4,128)(2,1)} %copy.55), calls=%async_computation.1 | async-start | bytes 4194304 | tf_op jit(solution)/shard_map/all_to_all | solution.py:56
  61.7 0.1 copy.64
  61.8 28.7 %all-to-all-done.1 = bf16[3,1024,256]{2,0,1:T(4,128)(2,1)S(1)} async-done(((bf16[3,1024,256]{2,0,1:T(4,128)(2,1)}), bf16[3,1024,256]{2,0,1:T(4,128)(2,1)S(1)}, u32[]{:S(2)}, u32[]{:S(2)}) %all-to-all-start.1) | async-done | bytes 1572896 | tf_op jit(solution)/shard_map/all_to_all | solution.py:56
  90.5 0.2 copy.56
  90.7 0.1 fusion.31
  90.8 0.2 copy.59
  91.0 0.2 copy.61
  91.2 0.2 copy.57
  91.4 4.3 %all-gather.5.cloned.1.call-done = bf16[1024,2,256]{0,2,1:T(8,128)(2,1)} async-done(((bf16[256,2,256]{0,2,1:T(8,128)(2,1)}), bf16[1024,2,256]{0,2,1:T(8,128)(2,1)}) %all-gather.5.cloned.1.call-update) | async-done | bytes 1048592 | tf_op jit(solution)/shard_map/all_gather | solution.py:42
  95.7 1.8 %convolution_bitcast_fusion.1 = f32[256,2,256]{0,2,1:T(8,128)S(1)} fusion(bf16[1024,2,256]{0,2,1:T(8,128)(2,1)} %all-gather.5.cloned.1.call-done, bf16[256,1024,1]{0,1,2:T(8,128)(2,1)S(1)} %bitcast.94), kind=kOutput, calls=%fused_computation.13 | convolution fusion | flops 268435456 | bytes 2097152 | tf_op jit(solution)/shard_map/dot_general | solution.py:28
  97.5 0.8 slice.57
  98.3 0.4 convolution_bitcast_fusion
  98.8 2.1 %fusion.12 = f32[2,256,512]{1,2,0:S(1)} fusion(bf16[2,256,512]{1,2,0:T(8,128)(2,1)S(1)} %bitcast.90, f32[256,2,256]{0,2,1:T(8,128)} %get-tuple-element.154, bf16[1024,2,256]{0,2,1:T(8,128)(2,1)S(1)} %copy-done, bf16[256,1024,1]{0,1,2:T(8,128)(2,1)S(1)} %bitcast.92, f32[256,2,192]{0,2,1:T(8,128)S(1)} %slice.59, f32[256,2,224]{0,2,1:T(8,128)} %slice.57), kind=kOutput, calls=%fused_computation.27 | convolution fusion | flops 403177472 | bytes 4521984
  100.8 0.0 copy-start.7
  100.9 0.0 copy-start.6
  100.9 0.1 convert_bitcast_fusion
  100.9 0.8 copy.65
  101.8 5.0 %all-to-all-start.2 = ((bf16[8,2,64,256]{3,2,1,0:T(8,128)(2,1)}), bf16[8,2,64,256]{3,2,1,0:T(8,128)(2,1)S(1)}, u32[]{:S(2)}, u32[]{:S(2)}) async-start(bf16[8,2,64,256]{3,2,1,0:T(8,128)(2,1)} %copy.65), calls=%async_computation.2 | async-start | bytes 1048576 | tf_op jit(solution)/shard_map/all_to_all | solution.py:71
  106.8 0.6 dynamic-slice
  108.1 0.2 dynamic-update-slice
  108.3 14.3 %all-reduce.4 = s32[16]{0:T(128)S(1)} all-reduce(s32[16]{0:T(128)S(1)} %dynamic-update-slice), channel_id=1, replica_groups=mesh['section'=4,'trial'=8] {'trial'}, use_global_device_ids=true, to_apply=%add.4 | all-reduce | flops 16 | bytes 128
  122.6 0.1 convert_reduce_fusion
  122.7 0.0 all-to-all-done.2
  122.7 0.3 copy.73
  123.0 9.4 %while.14 = (s32[]{:T(128)}, f32[8,16384]{1,0:T(8,128)S(1)}, s32[8]{0:T(128)S(1)}, s32[16]{0:T(128)S(1)}, f32[16,16384]{1,0:T(8,128)S(1)}, /*index=5*/s32[]{:T(128)}, s32[]{:T(128)}) while((s32[]{:T(128)}, f32[8,16384]{1,0:T(8,128)S(1)}, s32[8]{0:T(128)S(1)}, s32[16]{0:T(128)S(1)}, f32[16,16384]{1,0:T(8,128)S(1)}, ...), condition=%wide.region_2.3_spmd.clone, body=%wide.region_1.2_spmd.clone.sunk | while | flops 525451 | bytes 2625951 | solution.py:88
  123.1 0.6 gather_fusion.1
  123.7 0.7 gather_fusion
  124.5 0.1 select_add_fusion.2
  124.7 0.6 gather_fusion.1
  125.3 0.7 gather_fusion
  126.0 0.1 select_add_fusion.2
  126.2 0.6 gather_fusion.1
  126.9 0.7 gather_fusion
  127.6 0.1 select_add_fusion.2
  127.8 0.6 gather_fusion.1
  128.5 0.7 gather_fusion
  129.2 0.1 select_add_fusion.2
  129.4 0.6 gather_fusion.1
  130.0 0.7 gather_fusion
  130.8 0.1 select_add_fusion.2
  130.9 0.6 gather_fusion.1
  131.6 0.7 gather_fusion
  132.3 0.1 select_add_fusion.2
  132.5 0.8 copy.78
  (39 shorter events, 0.3 us)
Async XLA Ops:
  6.5 3.3 %copy-start.2 = (bf16[3,1024,256]{2,1,0:T(8,128)(2,1)S(1)}, bf16[3,1024,256]{2,1,0:T(8,128)(2,1)}, u32[]{:S(2)}) copy-start(bf16[3,1024,256]{2,1,0:T(8,128)(2,1)} %param.14) | copy-start | bytes 4718596
  6.5 44.9 %all-gather.3.cloned.1.call-start = ((), (), s32[]{:S(2)}) async-start(), calls=%async_computation.3 | async-start | bytes 1310720 | tf_op jit(solution)/shard_map/all_gather | solution.py:42
  12.6 5.3 %copy-start.5 = (bf16[256,2,256]{2,1,0:T(2,128)(2,1)S(1)}, bf16[256,2,256]{2,1,0:T(2,128)(2,1)}, u32[]{:S(2)}) copy-start(bf16[256,2,256]{2,1,0:T(2,128)(2,1)} %param.10) | copy-start | bytes 786436
  12.6 33.5 %all-to-all-start = ((bf16[3,1024,256]{2,0,1:T(4,128)(2,1)}), bf16[3,1024,256]{2,0,1:T(4,128)(2,1)S(1)}, u32[]{:S(2)}, u32[]{:S(2)}) async-start(bf16[3,1024,256]{2,0,1:T(4,128)(2,1)} %copy.52), calls=%async_computation | async-start | bytes 4194304 | tf_op jit(solution)/shard_map/all_to_all | solution.py:57
  17.9 77.9 %all-gather.5.cloned.1.call-start = ((), (), s32[]{:S(2)}) async-start(), calls=%async_computation.4 | async-start | bytes 1310720 | tf_op jit(solution)/shard_map/all_gather | solution.py:42
  51.4 1.8 %copy-start.1 = (bf16[1024,2,256]{0,2,1:T(8,128)(2,1)S(1)}, bf16[1024,2,256]{0,2,1:T(8,128)(2,1)}, u32[]{:S(2)}) copy-start(bf16[1024,2,256]{0,2,1:T(8,128)(2,1)} %all-gather.3.cloned.1.call-done) | copy-start | bytes 3145732
  53.8 1.5 %copy-start.3 = (bf16[3,1024,256]{2,1,0:T(8,128)(2,1)S(1)}, bf16[3,1024,256]{2,1,0:T(8,128)(2,1)}, u32[]{:S(2)}) copy-start(bf16[3,1024,256]{2,1,0:T(8,128)(2,1)} %param.13) | copy-start | bytes 4718596
  58.0 3.8 %copy-start.4 = (bf16[512,2,256]{2,1,0:T(2,128)(2,1)S(1)}, bf16[512,2,256]{2,1,0:T(2,128)(2,1)}, u32[]{:S(2)}) copy-start(bf16[512,2,256]{2,1,0:T(2,128)(2,1)} %param.9) | copy-start | bytes 1572868
  58.0 32.5 %all-to-all-start.1 = ((bf16[3,1024,256]{2,0,1:T(4,128)(2,1)}), bf16[3,1024,256]{2,0,1:T(4,128)(2,1)S(1)}, u32[]{:S(2)}, u32[]{:S(2)}) async-start(bf16[3,1024,256]{2,0,1:T(4,128)(2,1)} %copy.55), calls=%async_computation.1 | async-start | bytes 4194304 | tf_op jit(solution)/shard_map/all_to_all | solution.py:56
  95.7 2.6 %copy-start = (bf16[1024,2,256]{0,2,1:T(8,128)(2,1)S(1)}, bf16[1024,2,256]{0,2,1:T(8,128)(2,1)}, u32[]{:S(2)}) copy-start(bf16[1024,2,256]{0,2,1:T(8,128)(2,1)} %all-gather.5.cloned.1.call-done) | copy-start | bytes 3145732
  100.8 5.9 %copy-start.7 = (u32[32]{0:T(128)S(1)}, u32[32]{0:T(128)}, u32[]{:S(2)}) copy-start(u32[32]{0:T(128)} %constant.99) | copy-start | bytes 388
  100.9 7.2 %copy-start.6 = (s32[2]{0:T(128)S(1)}, s32[2]{0:T(128)}, u32[]{:S(2)}) copy-start(s32[2]{0:T(128)} %param.15) | copy-start | bytes 28
  101.8 20.9 %all-to-all-start.2 = ((bf16[8,2,64,256]{3,2,1,0:T(8,128)(2,1)}), bf16[8,2,64,256]{3,2,1,0:T(8,128)(2,1)S(1)}, u32[]{:S(2)}, u32[]{:S(2)}) async-start(bf16[8,2,64,256]{3,2,1,0:T(8,128)(2,1)} %copy.65), calls=%async_computation.2 | async-start | bytes 1048576 | tf_op jit(solution)/shard_map/all_to_all | solution.py:71
Sparse Core Ops, SparseCore 0:
  10.0 41.3 all-gather.2
  55.4 40.3 all-gather.4
where the time goes:
time: 141 us; the launch traced here: 140 us
  waiting for transfers between devices  63.2 us (45%)
  local copies, waits for them, and re-layouts  23.9 us (17%)
  blocking collectives  14.3 us (10%)
  between operations  14.3 us (10%)
  starting transfers between devices  14 us (10%)
  matrix products  7.97 us (6%)
  other arithmetic  2.09 us (1%)
    all_to_all x1, waiting for transfers between devices, body(): lax.all_to_all(first_kernel, 'section', split_axis=1, concat_axis=2, tile...  28.7 us
    all_to_all x1, waiting for transfers between devices, body(): lax.all_to_all(second_kernel, 'section', split_axis=1, concat_axis=2, til...  28.1 us
    unnamed x1, blocking collectives  14.3 us
    unnamed x26, local copies, waits for them, and re-layouts  9.83 us
    all_gather x2, waiting for transfers between devices, layer_backprop(): lax.all_gather(flow_grad, 'section', axis=0, tiled=True)  6.46 us
    dot_general x5, matrix products, tap_sum(): lax.dot_general(weights[kernel_tap], flow_grad, (((1,), (0,)), ((), ())),...  5.91 us
    all_to_all x1, starting transfers between devices, body(): lax.all_to_all(second_kernel, 'section', split_axis=1, concat_axis=2, til...  5.29 us
    all_to_all x1, starting transfers between devices, body(): lax.all_to_all(partials.astype(jnp.bfloat16), 'trial', split_axis=0, conc...  5.01 us
  transfers between devices with their start and end apart: 5, of which 4 were waited for; matrix products, arithmetic and copies ran while one was open for 8% of the time, Pallas kernels for 0%

commit v1 on v0

--- a/solution.py
+++ b/solution.py
@@ -1,8 +1,11 @@
+import functools
 import math
 
 import jax
 import jax.numpy as jnp
 from jax import lax
+from jax.experimental import pallas as pl
+from jax.experimental.pallas import tpu as pltpu
 from jax.sharding import PartitionSpec as P
 
 FIRST_DILATION = 32
@@ -91,6 +94,367 @@
     )
 
 
+MESH = pl.DeviceIdType.MESH
+TRIALS_HERE = 2
+
+
+def shifted(values, offset):
+    if offset == 0:
+        return values
+    width = values.shape[1]
+    rolled = pltpu.roll(values, width - offset, 1)
+    lane = lax.broadcasted_iota(jnp.int32, values.shape, 1)
+    return jnp.where(lane < width - offset, rolled, 0.0)
+
+
+def split_pairs(source, index, target, halves):
+    for chunk in range(halves):
+        mixed = source[pl.ds(chunk * 256, 256), :]
+        apart = jnp.dot(index, mixed, preferred_element_type=jnp.float32).astype(target.dtype)
+        for trial in range(TRIALS_HERE):
+            target[trial, pl.ds(chunk * 128, 128), :] = apart[trial * 128 : trial * 128 + 128]
+
+
+def fused(
+    shards,
+    spikes_hbm,
+    pre_one_in,
+    pre_two_in,
+    upstream_in,
+    kernel_one_hbm,
+    kernel_two_hbm,
+    ids_in,
+    out_ref,
+    kernels,
+    spikes_mixed,
+    spikes,
+    pre_one,
+    pre_two,
+    grad,
+    slope_one,
+    taps,
+    own,
+    wide,
+    outgoing,
+    diag_in,
+    side_in,
+    parts,
+    arrived,
+    ids_mine,
+    ids_all,
+    picks,
+    total,
+    load_sems,
+    diag_send,
+    diag_recv,
+    side_send,
+    side_recv,
+    part_send,
+    part_recv,
+    id_send,
+    id_recv,
+):
+    section = lax.axis_index("section")
+    me = lax.axis_index("trial")
+    along_x = section + 1 - 2 * (section % 2)
+    along_y = (section + 2) % 4
+    across = (along_x + 2) % 4
+    rows = parts.shape[1] // shards
+    spacings = (SECOND_DILATION, FIRST_DILATION)
+
+    loads = [
+        pltpu.make_async_copy(kernel_two_hbm, kernels.at[0], load_sems.at[0]),
+        pltpu.make_async_copy(kernel_one_hbm, kernels.at[1], load_sems.at[1]),
+        pltpu.make_async_copy(spikes_hbm, spikes_mixed, load_sems.at[2]),
+    ]
+    for load in loads:
+        load.start()
+
+    barrier = pltpu.get_barrier_semaphore()
+    for partner in (along_x, along_y):
+        pl.semaphore_signal(barrier, inc=1, device_id=(partner, me), device_id_type=MESH)
+    for step in range(1, shards):
+        peer = (me + step) % shards
+        pl.semaphore_signal(barrier, inc=1, device_id=(section, peer), device_id_type=MESH)
+
+    row = lax.broadcasted_iota(jnp.int32, (256, 256), 0)
+    column = lax.broadcasted_iota(jnp.int32, (256, 256), 1)
+    wanted = jnp.where(row < 128, 2 * row, 2 * row - 255)
+    index = (column == wanted).astype(jnp.float32).astype(jnp.bfloat16)
+
+    def diag_copies(unit):
+        return [
+            pltpu.make_async_remote_copy(
+                src_ref=outgoing.at[unit, 2, pl.ds(128 * way, 128)],
+                dst_ref=diag_in.at[unit, way],
+                send_sem=diag_send.at[unit, way],
+                recv_sem=diag_recv.at[unit, way],
+                device_id=(partner, me),
+                device_id_type=MESH,
+            )
+            for way, partner in enumerate((along_x, along_y))
+        ]
+
+    def side_copy(unit, way, half):
+        partner = (along_x, along_y)[way]
+        return pltpu.make_async_remote_copy(
+            src_ref=outgoing.at[unit, way, pl.ds(128 * half, 128)],
+            dst_ref=side_in.at[unit, way, pl.ds(128 * half, 128)],
+            send_sem=side_send.at[unit, way, half],
+            recv_sem=side_recv.at[unit, way, half],
+            device_id=(partner, me),
+            device_id_type=MESH,
+        )
+
+    def flow(layer, trial, upstream, slope):
+        rounded = (upstream * slope).astype(jnp.bfloat16).astype(jnp.float32)
+        for tap in range(3):
+            taps[tap] = shifted(rounded, tap * spacings[layer]).astype(jnp.bfloat16)
+
+    def product(layer, block, first, size):
+        result = None
+        for tap in range(3):
+            weights = kernels[layer, tap, pl.ds(pl.multiple_of(block * 256 + first, 128), size), :]
+            term = jnp.dot(weights, taps[tap], preferred_element_type=jnp.float32)
+            result = term if result is None else result + term
+        return result
+
+    def compute(layer, unit, now):
+        outgoing[unit, 2] = product(layer, across, 0, 256).astype(jnp.bfloat16)
+        if now:
+            for copy in diag_copies(unit):
+                copy.start()
+        outgoing[unit, 0, pl.ds(0, 128)] = product(layer, along_x, 0, 128).astype(jnp.bfloat16)
+        outgoing[unit, 1, pl.ds(128, 128)] = product(layer, along_y, 128, 128).astype(jnp.bfloat16)
+        if now:
+            side_copy(unit, 0, 0).start()
+            side_copy(unit, 1, 1).start()
+        wide[unit, 0] = product(layer, along_y, 0, 128)
+        wide[unit, 1] = product(layer, along_x, 128, 128)
+        own[unit] = product(layer, section, 0, 256)
+
+    def send(unit):
+        for copy in diag_copies(unit):
+            copy.start()
+        side_copy(unit, 0, 0).start()
+        side_copy(unit, 1, 1).start()
+
+    def forward(unit):
+        copies = diag_copies(unit)
+        for way in range(2):
+            copies[way].wait_recv()
+            target, half = 1 - way, way
+            joined = wide[unit, way] + diag_in[unit, way].astype(jnp.float32)
+            outgoing[unit, target, pl.ds(128 * half, 128)] = joined.astype(jnp.bfloat16)
+            side_copy(unit, target, half).start()
+
+    def finish(unit, trial):
+        for way in range(2):
+            for half in range(2):
+                side_copy(unit, way, half).wait_recv()
+        back = own[unit] + side_in[unit, 0].astype(jnp.float32) + side_in[unit, 1].astype(jnp.float32)
+        rounded = (grad[trial].astype(jnp.float32) + back).astype(jnp.bfloat16)
+        grad[trial] = rounded
+        return rounded
+
+    def part_copy(trial, step):
+        peer = (me + step) % shards
+        return pltpu.make_async_remote_copy(
+            src_ref=parts.at[trial, pl.ds(pl.multiple_of(peer * rows, rows), rows)],
+            dst_ref=arrived.at[trial, pl.ds(pl.multiple_of(me * rows, rows), rows)],
+            send_sem=part_send.at[trial, step],
+            recv_sem=part_recv.at[trial, step],
+            device_id=(section, peer),
+            device_id_type=MESH,
+        )
+
+    def id_copy(step):
+        peer = (me + step) % shards
+        return pltpu.make_async_remote_copy(
+            src_ref=ids_mine,
+            dst_ref=ids_all.at[me],
+            send_sem=id_send.at[step],
+            recv_sem=id_recv.at[step],
+            device_id=(section, peer),
+            device_id_type=MESH,
+        )
+
+    def readin(trial, gradient):
+        both = lax.dot_general(
+            spikes[trial], gradient, (((1,), (1,)), ((), ())), preferred_element_type=jnp.float32
+        )
+        parts[trial] = both.astype(jnp.bfloat16)
+        for step in range(1, shards):
+            part_copy(trial, step).start()
+        mine = pl.ds(pl.multiple_of(me * rows, rows), rows)
+        arrived[trial, mine] = parts[trial, mine]
+
+    def collect(trial):
+        for step in range(1, shards):
+            part_copy(trial, step).wait_recv()
+        return jnp.dot(picks[trial], arrived[trial], preferred_element_type=jnp.float32)
+
+    split_pairs(pre_two_in, index, pre_two, 2)
+    split_pairs(upstream_in, index, grad, 2)
+    flow(0, 0, grad[0].astype(jnp.float32), gelu_slope(pre_two[0]))
+    loads[0].wait()
+    pl.semaphore_wait(barrier, shards + 1)
+    compute(0, 0, True)
+
+    flow(0, 1, grad[1].astype(jnp.float32), gelu_slope(pre_two[1]))
+    compute(0, 1, False)
+    forward(0)
+    send(1)
+
+    top = lax.broadcasted_iota(jnp.int32, ids_mine.shape, 0)
+    ids_mine[...] = jnp.where(top == 0, ids_in[0], ids_in[1])
+    for step in range(1, shards):
+        id_copy(step).start()
+    ids_all[me] = ids_mine[...]
+
+    split_pairs(pre_one_in, index, pre_one, 2)
+    for trial in range(TRIALS_HERE):
+        slope_one[trial] = gelu_slope(pre_one[trial])
+    loads[1].wait()
+
+    flow(1, 0, finish(0, 0).astype(jnp.float32), slope_one[0])
+    compute(1, 2, False)
+    forward(1)
+    send(2)
+
+    loads[2].wait()
+    split_pairs(spikes_mixed, index, spikes, spikes_mixed.shape[0] // 256)
+
+    flow(1, 1, finish(1, 1).astype(jnp.float32), slope_one[1])
+    compute(1, 3, False)
+    forward(2)
+    send(3)
+
+    for step in range(1, shards):
+        id_copy(step).wait_recv()
+    line = lax.broadcasted_iota(jnp.int32, (shards * rows, 128), 0)
+    lane = lax.broadcasted_iota(jnp.int32, (shards * rows, 128), 1)
+    same = (line % rows) == (lane % rows)
+    session = line // rows
+    per = 128 // rows
+    for trial in range(TRIALS_HERE):
+        for piece in range(shards * rows // 128):
+            known = ids_all[piece * per, pl.ds(trial, 1), :]
+            for slot in range(1, per):
+                other = ids_all[piece * per + slot, pl.ds(trial, 1), :]
+                known = jnp.where(lane[:1] < slot * rows, known, other)
+            chosen = same & (session == known)
+            picks[trial, :, pl.ds(piece * 128, 128)] = chosen.astype(jnp.float32).astype(jnp.bfloat16)
+
+    readin(0, finish(2, 0))
+    forward(3)
+    readin(1, finish(3, 1))
+    total[...] = collect(0)
+    summed = total[...] + collect(1)
+    out_ref[...] = summed.astype(jnp.bfloat16).reshape(out_ref.shape)
+
+    for unit in range(4):
+        for copy in diag_copies(unit):
+            copy.wait_send()
+        for way in range(2):
+            for half in range(2):
+                side_copy(unit, way, half).wait_send()
+    for step in range(1, shards):
+        for trial in range(TRIALS_HERE):
+            part_copy(trial, step).wait_send()
+        id_copy(step).wait_send()
+
+
+def one_kernel(
+    spike_rates,
+    first_preactivation,
+    second_preactivation,
+    output_gradient,
+    first_kernel,
+    second_kernel,
+    session_of,
+):
+    shards = lax.axis_size("trial")
+    neurons, trials, steps = spike_rates.shape
+    block = output_gradient.shape[0]
+    rows = neurons // shards
+    f32, bf16 = jnp.float32, jnp.bfloat16
+    vmem = pl.BlockSpec(memory_space=pltpu.VMEM)
+    anywhere = pl.BlockSpec(memory_space=pl.ANY)
+    dma = pltpu.SemaphoreType.DMA
+
+    def pairs(array):
+        return array.reshape(array.shape[0] * trials, steps)
+
+    return pl.pallas_call(
+        functools.partial(fused, shards),
+        out_shape=jax.ShapeDtypeStruct((shards, rows, block), bf16),
+        in_specs=[
+            anywhere,
+            vmem,
+            vmem,
+            vmem,
+            anywhere,
+            anywhere,
+            pl.BlockSpec(memory_space=pltpu.SMEM),
+        ],
+        out_specs=vmem,
+        scratch_shapes=[
+            pltpu.VMEM((2,) + first_kernel.shape, bf16),
+            pltpu.VMEM((neurons * trials, steps), bf16),
+            pltpu.VMEM((trials, neurons, steps), bf16),
+            pltpu.VMEM((trials, block, steps), bf16),
+            pltpu.VMEM((trials, block, steps), bf16),
+            pltpu.VMEM((trials, block, steps), bf16),
+            pltpu.VMEM((trials, block, steps), f32),
+            pltpu.VMEM((3, block, steps), bf16),
+            pltpu.VMEM((4, block, steps), f32),
+            pltpu.VMEM((4, 2, block // 2, steps), f32),
+            pltpu.VMEM((4, 3, block, steps), bf16),
+            pltpu.VMEM((4, 2, block // 2, steps), bf16),
+            pltpu.VMEM((4, 2, block, steps), bf16),
+            pltpu.VMEM((trials, neurons, block), bf16),
+            pltpu.VMEM((trials, neurons, block), bf16),
+            pltpu.VMEM((8, 128), jnp.int32),
+            pltpu.VMEM((shards, 8, 128), jnp.int32),
+            pltpu.VMEM((trials, shards * rows, shards * rows), bf16),
+            pltpu.VMEM((shards * rows, block), f32),
+            dma((3,)),
+            dma((4, 2)),
+            dma((4, 2)),
+            dma((4, 2, 2)),
+            dma((4, 2, 2)),
+            dma((trials, shards)),
+            dma((trials, shards)),
+            dma((shards,)),
+            dma((shards,)),
+        ],
+        compiler_params=pltpu.CompilerParams(
+            collective_id=0, has_side_effects=True, vmem_limit_bytes=48 * 1024 * 1024
+        ),
+        cost_estimate=pl.CostEstimate(
+            flops=2_000_000_000, bytes_accessed=6_000_000, transcendentals=500_000
+        ),
+    )(
+        pairs(spike_rates),
+        pairs(first_preactivation),
+        pairs(second_preactivation),
+        pairs(output_gradient),
+        first_kernel,
+        second_kernel,
+        session_of,
+    )
+
+
+def choose(mesh, spike_rates, *others):
+    shards = mesh.shape["trial"]
+    neurons, trials, steps = spike_rates.shape
+    rows = neurons // shards
+    fits = mesh.shape["section"] == 4 and trials == TRIALS_HERE and steps == 256
+    fits = fits and others[0].shape[0] == 256 and neurons % 128 == 0 and rows in (16, 32, 64, 128)
+    return (one_kernel if fits else body)(spike_rates, *others)
+
+
 def solution(mesh):
     in_specs = (
         P(None, "trial", None),
@@ -102,4 +466,5 @@
         P("trial"),
     )
     out_specs = P(None, "trial", "section")
-    return jax.shard_map(body, mesh=mesh, in_specs=in_specs, out_specs=out_specs, check_vma=False)
+    run = functools.partial(choose, mesh)
+    return jax.shard_map(run, mesh=mesh, in_specs=in_specs, out_specs=out_specs, check_vma=False)

time: 141 us -> 41.3 us (0.29)
  waiting for transfers between devices: 63.2 us -> 0 us
  Pallas kernels: 0 us -> 34.3 us
  local copies, waits for them, and re-layouts: 23.9 us -> 6.63 us
  blocking collectives: 14.3 us -> 0 us
  between operations: 14.3 us -> 0.05 us
  starting transfers between devices: 14 us -> 0 us
  matrix products: 7.97 us -> 0 us
  other arithmetic: 2.09 us -> 0 us
    all_to_all x3 -> x0, waiting for transfers between devices: 56.7 us -> none  [the longest x1 28.7 us: body(): lax.all_to_all(first_kernel, 'section', split_axis=1, concat_axis=2, tile...]
    pallas_call x0 -> x1, Pallas kernels: none -> 34.3 us  [one_kernel(): pl.pallas_call(functools.partial(fused, shards), out_shape=jax.ShapeDtype...]
    unnamed x1 -> x0, blocking collectives: 14.3 us -> none
    all_to_all x3 -> x0, starting transfers between devices: 14 us -> none  [the longest x1 5.29 us: body(): lax.all_to_all(second_kernel, 'section', split_axis=1, concat_axis=2, til...]
    gather x12 -> x0, local copies, waits for them, and re-layouts: 8.18 us -> none  [the longest x6 4.32 us: add_offset(): rows_here = jnp.take(flat_parts, clipped, axis=0)]
    unnamed x26 -> x7, local copies, waits for them, and re-layouts: 9.83 us -> 2.12 us
    all_gather x2 -> x0, waiting for transfers between devices: 6.46 us -> none  [layer_backprop(): lax.all_gather(flow_grad, 'section', axis=0, tiled=True)]
    dot_general x5 -> x0, matrix products: 5.91 us -> none  [tap_sum(): lax.dot_general(weights[kernel_tap], flow_grad, (((1,), (0,)), ((), ())),...]
  transfers between devices with their start and end apart: 5 -> 0, of which waited for: 4 -> 0; matrix products, arithmetic and copies ran while one was open for 8% -> 0% of each run, Pallas kernels for 0% -> 0%
where the time goes in v1:
time: 41.3 us; the launch traced here: 41 us
  Pallas kernels  34.3 us (83%)
  local copies, waits for them, and re-layouts  6.63 us (16%)
    pallas_call x1, Pallas kernels, one_kernel(): pl.pallas_call(functools.partial(fused, shards), out_shape=jax.ShapeDtype...  34.3 us
    reshape x4, local copies, waits for them, and re-layouts, pairs(): return array.reshape(array.shape[0] * trials, steps)  4.52 us
    unnamed x7, local copies, waits for them, and re-layouts  2.12 us

profile of v1, /device:TPU:0, one launch (start us, length us, event | category | flops | bytes accessed | tf_op | source)
XLA Modules:
  0.0 41.0 jit_solution(4369089450220485090)
XLA Ops:
  0.0 0.0 copy-start.2
  0.0 0.0 copy-start
  0.0 1.2 %reshape.13.pre_one_in = bf16[512,256]{1,0:T(8,128)(2,1)S(1)} reshape(bf16[256,2,256]{2,1,0:T(2,128)(2,1)} %param.8) | data formatting | bytes 524288 | tf_op jit(solution)/shard_map/reshape | solution.py:387
  1.2 1.1 %reshape.14.pre_two_in = bf16[512,256]{1,0:T(8,128)(2,1)S(1)} reshape(bf16[256,2,256]{2,1,0:T(2,128)(2,1)} %param.9) | data formatting | bytes 524288 | tf_op jit(solution)/shard_map/reshape | solution.py:387
  2.2 1.1 %reshape.15.upstream_in = bf16[512,256]{1,0:T(8,128)(2,1)S(1)} reshape(bf16[256,2,256]{2,1,0:T(2,128)(2,1)} %param.10) | data formatting | bytes 524288 | tf_op jit(solution)/shard_map/reshape | solution.py:387
  3.3 1.2 %reshape.12.spikes_hbm = bf16[1024,256]{1,0:T(8,128)(2,1)S(1)} reshape(bf16[512,2,256]{2,1,0:T(2,128)(2,1)} %param.7) | data formatting | bytes 1048576 | tf_op jit(solution)/shard_map/reshape | solution.py:387
  4.5 0.0 copy-done.2
  4.5 0.0 copy-done
  4.6 0.0 copy-start.1
  4.6 1.4 %copy-done.1 = bf16[3,1024,256]{2,1,0:T(8,128)(2,1)S(1)} copy-done((bf16[3,1024,256]{2,1,0:T(8,128)(2,1)S(1)}, bf16[3,1024,256]{2,1,0:T(8,128)(2,1)}, u32[]{:S(2)}) %copy-start.1) | copy-done | bytes 1572888
  6.0 34.3 %shard_map.73 = bf16[8,64,256]{2,1,0:T(8,128)(2,1)S(1)} custom-call(bf16[1024,256]{1,0:T(8,128)(2,1)S(1)} %reshape.12.spikes_hbm, bf16[512,256]{1,0:T(8,128)(2,1)S(1)} %reshape.13.pre_one_in, bf16[512,256]{1,0:T(8,128)(2,1)S(1)} %reshape.14.pre_two_in, bf16[512,256]{1,0:T(8,128)(2,1)S(1)} %reshape.15.upstream_in, bf16[3,1024,256]{2,1,0:T(8,128)(2,1)S(1)} %copy-done, ...), custom_call_target="tpu_custom_call" | custom-call | flops 2000000000 | bytes 6000000 | tf_op jit(solution)/shard_map/pallas_call | solution.py:389
  40.3 0.7 %copy.9 = bf16[8,64,256]{2,1,0:T(8,128)(2,1)} copy(bf16[8,64,256]{2,1,0:T(8,128)(2,1)S(1)} %shard_map.73) | data formatting | bytes 524288
Async XLA Ops:
  0.0 4.5 %copy-start.2 = (s32[2]{0:T(128)S(1)}, s32[2]{0:T(128)}, u32[]{:S(2)}) copy-start(s32[2]{0:T(128)} %ids_in.1) | copy-start | bytes 28
  0.0 4.5 %copy-start = (bf16[3,1024,256]{2,1,0:T(8,128)(2,1)S(1)}, bf16[3,1024,256]{2,1,0:T(8,128)(2,1)}, u32[]{:S(2)}) copy-start(bf16[3,1024,256]{2,1,0:T(8,128)(2,1)} %kernel_one_hbm.1) | copy-start | bytes 4718596
  4.6 1.4 %copy-start.1 = (bf16[3,1024,256]{2,1,0:T(8,128)(2,1)S(1)}, bf16[3,1024,256]{2,1,0:T(8,128)(2,1)}, u32[]{:S(2)}) copy-start(bf16[3,1024,256]{2,1,0:T(8,128)(2,1)} %kernel_two_hbm.1) | copy-start | bytes 4718596

commit v2 on v1

--- a/solution.py
+++ b/solution.py
@@ -109,7 +109,7 @@
 
 def split_pairs(source, index, target, halves):
     for chunk in range(halves):
-        mixed = source[pl.ds(chunk * 256, 256), :]
+        mixed = source[pl.ds(chunk * 128, 128)].reshape(256, source.shape[2])
         apart = jnp.dot(index, mixed, preferred_element_type=jnp.float32).astype(target.dtype)
         for trial in range(TRIALS_HERE):
             target[trial, pl.ds(chunk * 128, 128), :] = apart[trial * 128 : trial * 128 + 128]
@@ -118,14 +118,17 @@
 def fused(
     shards,
     spikes_hbm,
-    pre_one_in,
-    pre_two_in,
-    upstream_in,
+    pre_one_hbm,
+    pre_two_hbm,
+    upstream_hbm,
     kernel_one_hbm,
     kernel_two_hbm,
     ids_in,
     out_ref,
     kernels,
+    pre_one_in,
+    pre_two_in,
+    upstream_in,
     spikes_mixed,
     spikes,
     pre_one,
@@ -159,13 +162,22 @@
     along_x = section + 1 - 2 * (section % 2)
     along_y = (section + 2) % 4
     across = (along_x + 2) % 4
-    rows = parts.shape[1] // shards
+    rows = parts.shape[2] // shards
     spacings = (SECOND_DILATION, FIRST_DILATION)
+    far_first = sorted(range(1, shards), key=lambda step: abs(2 * step - shards))
 
     loads = [
-        pltpu.make_async_copy(kernel_two_hbm, kernels.at[0], load_sems.at[0]),
-        pltpu.make_async_copy(kernel_one_hbm, kernels.at[1], load_sems.at[1]),
-        pltpu.make_async_copy(spikes_hbm, spikes_mixed, load_sems.at[2]),
+        pltpu.make_async_copy(source, target, load_sems.at[place])
+        for place, (source, target) in enumerate(
+            (
+                (pre_two_hbm, pre_two_in),
+                (upstream_hbm, upstream_in),
+                (kernel_two_hbm, kernels.at[0]),
+                (pre_one_hbm, pre_one_in),
+                (kernel_one_hbm, kernels.at[1]),
+                (spikes_hbm, spikes_mixed),
+            )
+        )
     ]
     for load in loads:
         load.start()
@@ -182,88 +194,88 @@
     wanted = jnp.where(row < 128, 2 * row, 2 * row - 255)
     index = (column == wanted).astype(jnp.float32).astype(jnp.bfloat16)
 
-    def diag_copies(unit):
-        return [
-            pltpu.make_async_remote_copy(
-                src_ref=outgoing.at[unit, 2, pl.ds(128 * way, 128)],
-                dst_ref=diag_in.at[unit, way],
-                send_sem=diag_send.at[unit, way],
-                recv_sem=diag_recv.at[unit, way],
-                device_id=(partner, me),
-                device_id_type=MESH,
-            )
-            for way, partner in enumerate((along_x, along_y))
-        ]
-
-    def side_copy(unit, way, half):
+    def diag_copy(unit, way, piece):
         partner = (along_x, along_y)[way]
         return pltpu.make_async_remote_copy(
-            src_ref=outgoing.at[unit, way, pl.ds(128 * half, 128)],
-            dst_ref=side_in.at[unit, way, pl.ds(128 * half, 128)],
-            send_sem=side_send.at[unit, way, half],
-            recv_sem=side_recv.at[unit, way, half],
+            src_ref=outgoing.at[unit, 2, pl.ds(128 * piece + 64 * way, 64)],
+            dst_ref=diag_in.at[unit, way, piece],
+            send_sem=diag_send.at[unit, way, piece],
+            recv_sem=diag_recv.at[unit, way, piece],
             device_id=(partner, me),
             device_id_type=MESH,
         )
 
-    def flow(layer, trial, upstream, slope):
+    def side_copy(unit, way, piece, half):
+        partner = (along_x, along_y)[way]
+        lines = pl.ds(128 * piece + 64 * half, 64)
+        return pltpu.make_async_remote_copy(
+            src_ref=outgoing.at[unit, way, lines],
+            dst_ref=side_in.at[unit, way, lines],
+            send_sem=side_send.at[unit, way, piece, half],
+            recv_sem=side_recv.at[unit, way, piece, half],
+            device_id=(partner, me),
+            device_id_type=MESH,
+        )
+
+    def flow(layer, lines, upstream, slope):
         rounded = (upstream * slope).astype(jnp.bfloat16).astype(jnp.float32)
         for tap in range(3):
-            taps[tap] = shifted(rounded, tap * spacings[layer]).astype(jnp.bfloat16)
-
-    def product(layer, block, first, size):
+            taps[tap, lines] = shifted(rounded, tap * spacings[layer]).astype(jnp.bfloat16)
+
+    def product(layer, target):
         result = None
         for tap in range(3):
-            weights = kernels[layer, tap, pl.ds(pl.multiple_of(block * 256 + first, 128), size), :]
+            weights = kernels[layer, tap, pl.ds(pl.multiple_of(target * 256, 256), 256), :]
             term = jnp.dot(weights, taps[tap], preferred_element_type=jnp.float32)
             result = term if result is None else result + term
         return result
 
-    def compute(layer, unit, now):
-        outgoing[unit, 2] = product(layer, across, 0, 256).astype(jnp.bfloat16)
-        if now:
-            for copy in diag_copies(unit):
-                copy.start()
-        outgoing[unit, 0, pl.ds(0, 128)] = product(layer, along_x, 0, 128).astype(jnp.bfloat16)
-        outgoing[unit, 1, pl.ds(128, 128)] = product(layer, along_y, 128, 128).astype(jnp.bfloat16)
-        if now:
-            side_copy(unit, 0, 0).start()
-            side_copy(unit, 1, 1).start()
-        wide[unit, 0] = product(layer, along_y, 0, 128)
-        wide[unit, 1] = product(layer, along_x, 128, 128)
-        own[unit] = product(layer, section, 0, 256)
-
-    def send(unit):
-        for copy in diag_copies(unit):
-            copy.start()
-        side_copy(unit, 0, 0).start()
-        side_copy(unit, 1, 1).start()
-
-    def forward(unit):
-        copies = diag_copies(unit)
+    def compute(layer, unit):
+        outgoing[unit, 2] = product(layer, across).astype(jnp.bfloat16)
+        for piece in range(2):
+            for way in range(2):
+                diag_copy(unit, way, piece).start()
+        for way, partner in enumerate((along_x, along_y)):
+            result = product(layer, partner)
+            for piece in range(2):
+                near, far = 128 * piece + 64 * way, 128 * piece + 64 * (1 - way)
+                outgoing[unit, way, pl.ds(near, 64)] = result[near : near + 64].astype(jnp.bfloat16)
+                wide[unit, 1 - way, piece] = result[far : far + 64]
+                side_copy(unit, way, piece, way).start()
+        own[unit] = product(layer, section)
+
+    def forward(unit, piece):
         for way in range(2):
-            copies[way].wait_recv()
-            target, half = 1 - way, way
-            joined = wide[unit, way] + diag_in[unit, way].astype(jnp.float32)
-            outgoing[unit, target, pl.ds(128 * half, 128)] = joined.astype(jnp.bfloat16)
-            side_copy(unit, target, half).start()
-
-    def finish(unit, trial):
+            diag_copy(unit, way, piece).wait_recv()
+            joined = wide[unit, way, piece] + diag_in[unit, way, piece].astype(jnp.float32)
+            lines = pl.ds(128 * piece + 64 * way, 64)
+            outgoing[unit, 1 - way, lines] = joined.astype(jnp.bfloat16)
+            side_copy(unit, 1 - way, piece, way).start()
+
+    def finish(unit, trial, piece):
         for way in range(2):
             for half in range(2):
-                side_copy(unit, way, half).wait_recv()
-        back = own[unit] + side_in[unit, 0].astype(jnp.float32) + side_in[unit, 1].astype(jnp.float32)
-        rounded = (grad[trial].astype(jnp.float32) + back).astype(jnp.bfloat16)
-        grad[trial] = rounded
+                side_copy(unit, way, piece, half).wait_recv()
+        lines = pl.ds(128 * piece, 128)
+        first, second = side_in[unit, 0, lines], side_in[unit, 1, lines]
+        back = own[unit, lines] + first.astype(jnp.float32) + second.astype(jnp.float32)
+        rounded = (grad[trial, lines].astype(jnp.float32) + back).astype(jnp.bfloat16)
+        grad[trial, lines] = rounded
         return rounded
 
-    def part_copy(trial, step):
+    def turn(unit, trial):
+        for piece in range(2):
+            lines = pl.ds(128 * piece, 128)
+            upstream = finish(unit, trial, piece).astype(jnp.float32)
+            flow(1, lines, upstream, slope_one[trial, lines])
+
+    def part_copy(trial, piece, step):
         peer = (me + step) % shards
         return pltpu.make_async_remote_copy(
-            src_ref=parts.at[trial, pl.ds(pl.multiple_of(peer * rows, rows), rows)],
-            dst_ref=arrived.at[trial, pl.ds(pl.multiple_of(me * rows, rows), rows)],
-            send_sem=part_send.at[trial, step],
-            recv_sem=part_recv.at[trial, step],
+            src_ref=parts.at[trial, piece, pl.ds(pl.multiple_of(peer * rows, rows), rows)],
+            dst_ref=arrived.at[trial, piece, pl.ds(pl.multiple_of(me * rows, rows), rows)],
+            send_sem=part_send.at[trial, piece, step],
+            recv_sem=part_recv.at[trial, piece, step],
             device_id=(section, peer),
             device_id_type=MESH,
         )
@@ -279,32 +291,35 @@
             device_id_type=MESH,
         )
 
-    def readin(trial, gradient):
+    def readin(trial, piece, gradient):
         both = lax.dot_general(
             spikes[trial], gradient, (((1,), (1,)), ((), ())), preferred_element_type=jnp.float32
         )
-        parts[trial] = both.astype(jnp.bfloat16)
+        parts[trial, piece] = both.astype(jnp.bfloat16)
+        for step in far_first:
+            part_copy(trial, piece, step).start()
+        mine = pl.ds(pl.multiple_of(me * rows, rows), rows)
+        arrived[trial, piece, mine] = parts[trial, piece, mine]
+
+    def collect(trial, piece):
         for step in range(1, shards):
-            part_copy(trial, step).start()
-        mine = pl.ds(pl.multiple_of(me * rows, rows), rows)
-        arrived[trial, mine] = parts[trial, mine]
-
-    def collect(trial):
-        for step in range(1, shards):
-            part_copy(trial, step).wait_recv()
-        return jnp.dot(picks[trial], arrived[trial], preferred_element_type=jnp.float32)
-
+            part_copy(trial, piece, step).wait_recv()
+        return jnp.dot(picks[trial], arrived[trial, piece], preferred_element_type=jnp.float32)
+
+    whole = pl.ds(0, 256)
+    loads[0].wait()
     split_pairs(pre_two_in, index, pre_two, 2)
+    loads[1].wait()
     split_pairs(upstream_in, index, grad, 2)
-    flow(0, 0, grad[0].astype(jnp.float32), gelu_slope(pre_two[0]))
-    loads[0].wait()
+    flow(0, whole, grad[0].astype(jnp.float32), gelu_slope(pre_two[0]))
+    loads[2].wait()
     pl.semaphore_wait(barrier, shards + 1)
-    compute(0, 0, True)
-
-    flow(0, 1, grad[1].astype(jnp.float32), gelu_slope(pre_two[1]))
-    compute(0, 1, False)
-    forward(0)
-    send(1)
+    compute(0, 0)
+
+    flow(0, whole, grad[1].astype(jnp.float32), gelu_slope(pre_two[1]))
+    forward(0, 0)
+    forward(0, 1)
+    compute(0, 1)
 
     top = lax.broadcasted_iota(jnp.int32, ids_mine.shape, 0)
     ids_mine[...] = jnp.where(top == 0, ids_in[0], ids_in[1])
@@ -312,23 +327,29 @@
         id_copy(step).start()
     ids_all[me] = ids_mine[...]
 
+    loads[3].wait()
     split_pairs(pre_one_in, index, pre_one, 2)
     for trial in range(TRIALS_HERE):
         slope_one[trial] = gelu_slope(pre_one[trial])
-    loads[1].wait()
-
-    flow(1, 0, finish(0, 0).astype(jnp.float32), slope_one[0])
-    compute(1, 2, False)
-    forward(1)
-    send(2)
-
-    loads[2].wait()
-    split_pairs(spikes_mixed, index, spikes, spikes_mixed.shape[0] // 256)
-
-    flow(1, 1, finish(1, 1).astype(jnp.float32), slope_one[1])
-    compute(1, 3, False)
-    forward(2)
-    send(3)
+    forward(1, 0)
+    forward(1, 1)
+
+    loads[4].wait()
+    turn(0, 0)
+    compute(1, 2)
+
+    turn(1, 1)
+    forward(2, 0)
+    forward(2, 1)
+    compute(1, 3)
+
+    loads[5].wait()
+    split_pairs(spikes_mixed, index, spikes, spikes_mixed.shape[0] // 128)
+
+    readin(0, 0, finish(2, 0, 0))
+    forward(3, 0)
+    forward(3, 1)
+    readin(0, 1, finish(2, 0, 1))
 
     for step in range(1, shards):
         id_copy(step).wait_recv()
@@ -346,22 +367,24 @@
             chosen = same & (session == known)
             picks[trial, :, pl.ds(piece * 128, 128)] = chosen.astype(jnp.float32).astype(jnp.bfloat16)
 
-    readin(0, finish(2, 0))
-    forward(3)
-    readin(1, finish(3, 1))
-    total[...] = collect(0)
-    summed = total[...] + collect(1)
-    out_ref[...] = summed.astype(jnp.bfloat16).reshape(out_ref.shape)
-
-    for unit in range(4):
-        for copy in diag_copies(unit):
-            copy.wait_send()
-        for way in range(2):
-            for half in range(2):
-                side_copy(unit, way, half).wait_send()
+    for piece in range(2):
+        readin(1, piece, finish(3, 1, piece))
+    for piece in range(2):
+        total[piece] = collect(0, piece)
+    for piece in range(2):
+        summed = (total[piece] + collect(1, piece)).astype(jnp.bfloat16)
+        out_ref[:, :, pl.ds(128 * piece, 128)] = summed.reshape(shards, rows, 128)
+
+    for piece in range(2):
+        for unit in range(4):
+            for way in range(2):
+                diag_copy(unit, way, piece).wait_send()
+                for half in range(2):
+                    side_copy(unit, way, piece, half).wait_send()
+        for step in range(1, shards):
+            for trial in range(TRIALS_HERE):
+                part_copy(trial, piece, step).wait_send()
     for step in range(1, shards):
-        for trial in range(TRIALS_HERE):
-            part_copy(trial, step).wait_send()
         id_copy(step).wait_send()
 
 
@@ -380,28 +403,28 @@
     rows = neurons // shards
     f32, bf16 = jnp.float32, jnp.bfloat16
     vmem = pl.BlockSpec(memory_space=pltpu.VMEM)
-    anywhere = pl.BlockSpec(memory_space=pl.ANY)
+    hbm = pl.BlockSpec(memory_space=pltpu.HBM)
     dma = pltpu.SemaphoreType.DMA
-
-    def pairs(array):
-        return array.reshape(array.shape[0] * trials, steps)
 
     return pl.pallas_call(
         functools.partial(fused, shards),
         out_shape=jax.ShapeDtypeStruct((shards, rows, block), bf16),
         in_specs=[
-            anywhere,
-            vmem,
-            vmem,
-            vmem,
-            anywhere,
-            anywhere,
+            hbm,
+            hbm,
+            hbm,
+            hbm,
+            hbm,
+            hbm,
             pl.BlockSpec(memory_space=pltpu.SMEM),
         ],
         out_specs=vmem,
         scratch_shapes=[
             pltpu.VMEM((2,) + first_kernel.shape, bf16),
-            pltpu.VMEM((neurons * trials, steps), bf16),
+            pltpu.VMEM((block, trials, steps), bf16),
+            pltpu.VMEM((block, trials, steps), bf16),
+            pltpu.VMEM((block, trials, steps), bf16),
+            pltpu.VMEM((neurons, trials, steps), bf16),
             pltpu.VMEM((trials, neurons, steps), bf16),
             pltpu.VMEM((trials, block, steps), bf16),
             pltpu.VMEM((trials, block, steps), bf16),
@@ -409,37 +432,37 @@
             pltpu.VMEM((trials, block, steps), f32),
             pltpu.VMEM((3, block, steps), bf16),
             pltpu.VMEM((4, block, steps), f32),
-            pltpu.VMEM((4, 2, block // 2, steps), f32),
+            pltpu.VMEM((4, 2, 2, block // 4, steps), f32),
             pltpu.VMEM((4, 3, block, steps), bf16),
-            pltpu.VMEM((4, 2, block // 2, steps), bf16),
+            pltpu.VMEM((4, 2, 2, block // 4, steps), bf16),
             pltpu.VMEM((4, 2, block, steps), bf16),
-            pltpu.VMEM((trials, neurons, block), bf16),
-            pltpu.VMEM((trials, neurons, block), bf16),
+            pltpu.VMEM((trials, 2, neurons, block // 2), bf16),
+            pltpu.VMEM((trials, 2, neurons, block // 2), bf16),
             pltpu.VMEM((8, 128), jnp.int32),
             pltpu.VMEM((shards, 8, 128), jnp.int32),
             pltpu.VMEM((trials, shards * rows, shards * rows), bf16),
-            pltpu.VMEM((shards * rows, block), f32),
-            dma((3,)),
-            dma((4, 2)),
-            dma((4, 2)),
+            pltpu.VMEM((2, shards * rows, block // 2), f32),
+            dma((6,)),
             dma((4, 2, 2)),
             dma((4, 2, 2)),
-            dma((trials, shards)),
-            dma((trials, shards)),
+            dma((4, 2, 2, 2)),
+            dma((4, 2, 2, 2)),
+            dma((trials, 2, shards)),
+            dma((trials, 2, shards)),
             dma((shards,)),
             dma((shards,)),
         ],
         compiler_params=pltpu.CompilerParams(
-            collective_id=0, has_side_effects=True, vmem_limit_bytes=48 * 1024 * 1024
+            collective_id=0, has_side_effects=True, vmem_limit_bytes=63 * 1024 * 1024
         ),
         cost_estimate=pl.CostEstimate(
             flops=2_000_000_000, bytes_accessed=6_000_000, transcendentals=500_000
         ),
     )(
-        pairs(spike_rates),
-        pairs(first_preactivation),
-        pairs(second_preactivation),
-        pairs(output_gradient),
+        spike_rates,
+        first_preactivation,
+        second_preactivation,
+        output_gradient,
         first_kernel,
         second_kernel,
         session_of,

time: 41.3 us -> 37.6 us (0.910)
  local copies, waits for them, and re-layouts: 6.63 us -> 1.67 us
  Pallas kernels: 34.3 us -> 35.8 us
    reshape x4 -> x0, local copies, waits for them, and re-layouts: 4.52 us -> none  [pairs(): return array.reshape(array.shape[0] * trials, steps)]
    pallas_call x1, Pallas kernels: 34.3 us -> 35.8 us  [one_kernel(): pl.pallas_call(functools.partial(fused, shards), out_shape=jax.ShapeDtype...]
    unnamed x7 -> x1, local copies, waits for them, and re-layouts: 2.12 us -> 1.67 us
where the time goes in v2:
time: 37.6 us; the launch traced here: 37.4 us
  Pallas kernels  35.8 us (95%)
  local copies, waits for them, and re-layouts  1.67 us (4%)
    pallas_call x1, Pallas kernels, one_kernel(): pl.pallas_call(functools.partial(fused, shards), out_shape=jax.ShapeDtype...  35.8 us
    unnamed x1, local copies, waits for them, and re-layouts  1.67 us

profile of v2, /device:TPU:0, one launch (start us, length us, event | category | flops | bytes accessed | tf_op | source)
XLA Modules:
  0.0 37.4 jit_solution(10475298382472669022)
XLA Ops:
  0.0 35.8 %shard_map.73 = bf16[8,64,256]{2,1,0:T(8,128)(2,1)} custom-call(bf16[512,2,256]{2,1,0:T(2,128)(2,1)} %spikes_hbm.1, bf16[256,2,256]{2,1,0:T(2,128)(2,1)} %pre_one_hbm.1, bf16[256,2,256]{2,1,0:T(2,128)(2,1)} %pre_two_hbm.1, bf16[256,2,256]{2,1,0:T(2,128)(2,1)} %upstream_hbm.1, bf16[3,1024,256]{2,1,0:T(8,128)(2,1)} %kernel_one_hbm.1, ...), custom_call_target="tpu_custom_call" | custom-call | flops 2000000000 | bytes 6000000 | tf_op jit(solution)/shard_map/pallas_call | solution.py:409
  35.8 1.7 %copy.9 = bf16[8,64,256]{2,1,0:T(8,128)(2,1)} copy(bf16[8,64,256]{2,1,0:T(8,128)(2,1)} %shard_map.73) | data formatting | bytes 524288

commit v3 on v2

--- a/solution.py
+++ b/solution.py
@@ -232,16 +232,17 @@
 
     def compute(layer, unit):
         outgoing[unit, 2] = product(layer, across).astype(jnp.bfloat16)
-        for piece in range(2):
-            for way in range(2):
-                diag_copy(unit, way, piece).start()
+        for way in range(2):
+            diag_copy(unit, way, 0).start()
         for way, partner in enumerate((along_x, along_y)):
             result = product(layer, partner)
             for piece in range(2):
                 near, far = 128 * piece + 64 * way, 128 * piece + 64 * (1 - way)
                 outgoing[unit, way, pl.ds(near, 64)] = result[near : near + 64].astype(jnp.bfloat16)
                 wide[unit, 1 - way, piece] = result[far : far + 64]
-                side_copy(unit, way, piece, way).start()
+            side_copy(unit, way, 0, way).start()
+            diag_copy(unit, way, 1).start()
+            side_copy(unit, way, 1, way).start()
         own[unit] = product(layer, section)
 
     def forward(unit, piece):
@@ -318,38 +319,34 @@
 
     flow(0, whole, grad[1].astype(jnp.float32), gelu_slope(pre_two[1]))
     forward(0, 0)
-    forward(0, 1)
-    compute(0, 1)
-
     top = lax.broadcasted_iota(jnp.int32, ids_mine.shape, 0)
     ids_mine[...] = jnp.where(top == 0, ids_in[0], ids_in[1])
     for step in range(1, shards):
         id_copy(step).start()
     ids_all[me] = ids_mine[...]
-
     loads[3].wait()
     split_pairs(pre_one_in, index, pre_one, 2)
-    for trial in range(TRIALS_HERE):
-        slope_one[trial] = gelu_slope(pre_one[trial])
-    forward(1, 0)
-    forward(1, 1)
-
+    slope_one[0] = gelu_slope(pre_one[0])
+    forward(0, 1)
+    compute(0, 1)
+
+    slope_one[1] = gelu_slope(pre_one[1])
     loads[4].wait()
     turn(0, 0)
     compute(1, 2)
-
-    turn(1, 1)
+    forward(1, 0)
+    loads[5].wait()
+    split_pairs(spikes_mixed, index, spikes, spikes_mixed.shape[0] // 128)
     forward(2, 0)
     forward(2, 1)
+    forward(1, 1)
+
+    readin(0, 0, finish(2, 0, 0))
+    readin(0, 1, finish(2, 0, 1))
+    turn(1, 1)
     compute(1, 3)
-
-    loads[5].wait()
-    split_pairs(spikes_mixed, index, spikes, spikes_mixed.shape[0] // 128)
-
-    readin(0, 0, finish(2, 0, 0))
     forward(3, 0)
     forward(3, 1)
-    readin(0, 1, finish(2, 0, 1))
 
     for step in range(1, shards):
         id_copy(step).wait_recv()

time: 37.6 us -> 39.3 us (1.045)
  Pallas kernels: 35.8 us -> 37.4 us
    pallas_call x1, Pallas kernels: 35.8 us -> 37.4 us  [one_kernel(): pl.pallas_call(functools.partial(fused, shards), out_shape=jax.ShapeDtype...]
where the time goes in v3:
time: 39.3 us; the launch traced here: 39.1 us
  Pallas kernels  37.4 us (95%)
  local copies, waits for them, and re-layouts  1.67 us (4%)
    pallas_call x1, Pallas kernels, one_kernel(): pl.pallas_call(functools.partial(fused, shards), out_shape=jax.ShapeDtype...  37.4 us
    unnamed x1, local copies, waits for them, and re-layouts  1.67 us

profile of v3, /device:TPU:0, one launch (start us, length us, event | category | flops | bytes accessed | tf_op | source)
XLA Modules:
  0.0 39.1 jit_solution(7864907043741625561)
XLA Ops:
  0.0 37.4 %shard_map.73 = bf16[8,64,256]{2,1,0:T(8,128)(2,1)} custom-call(bf16[512,2,256]{2,1,0:T(2,128)(2,1)} %spikes_hbm.1, bf16[256,2,256]{2,1,0:T(2,128)(2,1)} %pre_one_hbm.1, bf16[256,2,256]{2,1,0:T(2,128)(2,1)} %pre_two_hbm.1, bf16[256,2,256]{2,1,0:T(2,128)(2,1)} %upstream_hbm.1, bf16[3,1024,256]{2,1,0:T(8,128)(2,1)} %kernel_one_hbm.1, ...), custom_call_target="tpu_custom_call" | custom-call | flops 2000000000 | bytes 6000000 | tf_op jit(solution)/shard_map/pallas_call | solution.py:406
  37.4 1.7 %copy.9 = bf16[8,64,256]{2,1,0:T(8,128)(2,1)} copy(bf16[8,64,256]{2,1,0:T(8,128)(2,1)} %shard_map.73) | data formatting | bytes 524288

commit v4 on v2

--- a/solution.py
+++ b/solution.py
@@ -109,7 +109,7 @@
 
 def split_pairs(source, index, target, halves):
     for chunk in range(halves):
-        mixed = source[pl.ds(chunk * 128, 128)].reshape(256, source.shape[2])
+        mixed = source[pl.ds(chunk * 256, 256), :]
         apart = jnp.dot(index, mixed, preferred_element_type=jnp.float32).astype(target.dtype)
         for trial in range(TRIALS_HERE):
             target[trial, pl.ds(chunk * 128, 128), :] = apart[trial * 128 : trial * 128 + 128]
@@ -170,12 +170,12 @@
         pltpu.make_async_copy(source, target, load_sems.at[place])
         for place, (source, target) in enumerate(
             (
-                (pre_two_hbm, pre_two_in),
-                (upstream_hbm, upstream_in),
+                (pre_two_hbm.reshape(pre_two_in.shape), pre_two_in),
+                (upstream_hbm.reshape(upstream_in.shape), upstream_in),
                 (kernel_two_hbm, kernels.at[0]),
-                (pre_one_hbm, pre_one_in),
+                (pre_one_hbm.reshape(pre_one_in.shape), pre_one_in),
                 (kernel_one_hbm, kernels.at[1]),
-                (spikes_hbm, spikes_mixed),
+                (spikes_hbm.reshape(spikes_mixed.shape), spikes_mixed),
             )
         )
     ]
@@ -344,7 +344,7 @@
     compute(1, 3)
 
     loads[5].wait()
-    split_pairs(spikes_mixed, index, spikes, spikes_mixed.shape[0] // 128)
+    split_pairs(spikes_mixed, index, spikes, spikes_mixed.shape[0] // 256)
 
     readin(0, 0, finish(2, 0, 0))
     forward(3, 0)
@@ -421,10 +421,10 @@
         out_specs=vmem,
         scratch_shapes=[
             pltpu.VMEM((2,) + first_kernel.shape, bf16),
-            pltpu.VMEM((block, trials, steps), bf16),
-            pltpu.VMEM((block, trials, steps), bf16),
-            pltpu.VMEM((block, trials, steps), bf16),
-            pltpu.VMEM((neurons, trials, steps), bf16),
+            pltpu.VMEM((block * trials, steps), bf16),
+            pltpu.VMEM((block * trials, steps), bf16),
+            pltpu.VMEM((block * trials, steps), bf16),
+            pltpu.VMEM((neurons * trials, steps), bf16),
             pltpu.VMEM((trials, neurons, steps), bf16),
             pltpu.VMEM((trials, block, steps), bf16),
             pltpu.VMEM((trials, block, steps), bf16),

time: 37.6 us -> 37.6 us (level)
  no operation moved by 1% of the time
where the time goes in v4:
time: 37.6 us; the launch traced here: 37.5 us
  Pallas kernels  35.8 us (95%)
  local copies, waits for them, and re-layouts  1.67 us (4%)
    pallas_call x1, Pallas kernels, one_kernel(): pl.pallas_call(functools.partial(fused, shards), out_shape=jax.ShapeDtype...  35.8 us
    unnamed x1, local copies, waits for them, and re-layouts  1.67 us

profile of v4, /device:TPU:0, one launch (start us, length us, event | category | flops | bytes accessed | tf_op | source)
XLA Modules:
  0.0 37.5 jit_solution(11295821819595788682)
XLA Ops:
  0.0 35.8 %shard_map.73 = bf16[8,64,256]{2,1,0:T(8,128)(2,1)} custom-call(bf16[512,2,256]{2,1,0:T(2,128)(2,1)} %spikes_hbm.1, bf16[256,2,256]{2,1,0:T(2,128)(2,1)} %pre_one_hbm.1, bf16[256,2,256]{2,1,0:T(2,128)(2,1)} %pre_two_hbm.1, bf16[256,2,256]{2,1,0:T(2,128)(2,1)} %upstream_hbm.1, bf16[3,1024,256]{2,1,0:T(8,128)(2,1)} %kernel_one_hbm.1, ...), custom_call_target="tpu_custom_call" | custom-call | flops 2000000000 | bytes 6000000 | tf_op jit(solution)/shard_map/pallas_call | solution.py:409
  35.8 1.7 %copy.9 = bf16[8,64,256]{2,1,0:T(8,128)(2,1)} copy(bf16[8,64,256]{2,1,0:T(8,128)(2,1)} %shard_map.73) | data formatting | bytes 524288

commit v5 on v4

--- a/solution.py
+++ b/solution.py
@@ -329,8 +329,7 @@
 
     loads[3].wait()
     split_pairs(pre_one_in, index, pre_one, 2)
-    for trial in range(TRIALS_HERE):
-        slope_one[trial] = gelu_slope(pre_one[trial])
+    slope_one[0] = gelu_slope(pre_one[0])
     forward(1, 0)
     forward(1, 1)
 
@@ -338,6 +337,7 @@
     turn(0, 0)
     compute(1, 2)
 
+    slope_one[1] = gelu_slope(pre_one[1])
     turn(1, 1)
     forward(2, 0)
     forward(2, 1)
@@ -408,7 +408,7 @@
 
     return pl.pallas_call(
         functools.partial(fused, shards),
-        out_shape=jax.ShapeDtypeStruct((shards, rows, block), bf16),
+        out_shape=pltpu.VMEM((shards, rows, block), bf16),
         in_specs=[
             hbm,
             hbm,
@@ -453,7 +453,7 @@
             dma((shards,)),
         ],
         compiler_params=pltpu.CompilerParams(
-            collective_id=0, has_side_effects=True, vmem_limit_bytes=63 * 1024 * 1024
+            collective_id=0, has_side_effects=True, vmem_limit_bytes=60 * 1024 * 1024
         ),
         cost_estimate=pl.CostEstimate(
             flops=2_000_000_000, bytes_accessed=6_000_000, transcendentals=500_000

time: 37.6 us -> 36 us (0.957)
  local copies, waits for them, and re-layouts: 1.67 us -> 0.71 us
  Pallas kernels: 35.8 us -> 35.1 us
    unnamed x1, local copies, waits for them, and re-layouts: 1.67 us -> 0.71 us
    pallas_call x1, Pallas kernels: 35.8 us -> 35.1 us  [one_kernel(): pl.pallas_call(functools.partial(fused, shards), out_shape=pltpu.VMEM((sh...]
where the time goes in v5:
time: 36 us; the launch traced here: 35.8 us
  Pallas kernels  35.1 us (98%)
  local copies, waits for them, and re-layouts  0.71 us (2%)
    pallas_call x1, Pallas kernels, one_kernel(): pl.pallas_call(functools.partial(fused, shards), out_shape=pltpu.VMEM((sh...  35.1 us

profile of v5, /device:TPU:0, one launch (start us, length us, event | category | flops | bytes accessed | tf_op | source)
XLA Modules:
  0.0 35.8 jit_solution(15283881481269474078)
XLA Ops:
  0.0 35.1 %shard_map.73 = bf16[8,64,256]{2,1,0:T(8,128)(2,1)S(1)} custom-call(bf16[512,2,256]{2,1,0:T(2,128)(2,1)} %spikes_hbm.1, bf16[256,2,256]{2,1,0:T(2,128)(2,1)} %pre_one_hbm.1, bf16[256,2,256]{2,1,0:T(2,128)(2,1)} %pre_two_hbm.1, bf16[256,2,256]{2,1,0:T(2,128)(2,1)} %upstream_hbm.1, bf16[3,1024,256]{2,1,0:T(8,128)(2,1)} %kernel_one_hbm.1, ...), custom_call_target="tpu_custom_call" | custom-call | flops 2000000000 | bytes 6000000 | tf_op jit(solution)/shard_map/pallas_call | solution.py:409
  35.1 0.7 %copy.9 = bf16[8,64,256]{2,1,0:T(8,128)(2,1)} copy(bf16[8,64,256]{2,1,0:T(8,128)(2,1)S(1)} %shard_map.73) | data formatting | bytes 524288
